TPU v7x, 32 devices: a whole 2x2x4 slice. The times are simulated.
32 devices in a mesh: groups: 2 (over x), context: 16 (over z, y, core).
Axes of the slice: x: 2, y: 2, z: 4, core: 2. Of those that a mesh axis runs over, the one named last changes fastest.
Arguments:
- grad_out: bfloat16 [4096, 8192], P(('groups', 'context')), parts along dimension 0, may hold values from -0.125 to 0.125
- saved: bfloat16 [4096, 8192], P(('groups', 'context')), parts along dimension 0, may hold values from -6 to 6
- block_route: int32 [32, 16], P('groups'), parts along dimension 0, may hold values from 0 to 15, each once within a row
Outputs:
- weight_grad: bfloat16 [16384, 8192], P(('groups', 'context')), parts along dimension 0
There are 2 independent parts, one for each index of `groups`. A program takes and returns all parts, laid end to end along the dimension named above; each array names one. Nothing has to cross between parts.
Inputs may be any that keep to these rules, and one draw needn't show every extreme that they name: Each row of block_route is a permutation of 0 to 15.
All inputs are finite; a program needn't handle non-finite values.
Results may differ from a plain program's by a relative error of at most 0.001.
Values may be sent and summed in bfloat16 or wider, within the bound.
A program may use at most 128 MiB of HBM per device.

v0:
```python
import math

import jax
import jax.numpy as jnp
from jax import lax
from jax.sharding import PartitionSpec as P


def partner(array, axis, apart):
    return lax.ppermute(array, axis, [(i, i ^ 1 << apart) for i in range(lax.axis_size(axis))])


def routed_order(block_route, devices, tok_rows, blocksize):
    sources = jnp.arange(devices, dtype=jnp.int32)
    starts = sources[None, :] * tok_rows + block_route.T * blocksize
    offsets = jnp.arange(blocksize, dtype=jnp.int32)
    return (starts[:, :, None] + offsets[None, None, :]).reshape(-1)


def join_pair(mine, other, upper, axis_dim):
    lower_first = jnp.concatenate((mine, other), axis=axis_dim)
    upper_first = jnp.concatenate((other, mine), axis=axis_dim)
    return jnp.where(upper, upper_first, lower_first)


def body(grad_out, saved, block_route):
    devices = lax.axis_size("context")
    side = math.isqrt(devices)
    levels = side.bit_length() - 1
    myself = lax.axis_index("context")
    tok_rows, width = grad_out.shape
    inner = saved.shape[1]
    blocksize = tok_rows // devices
    head_piece = inner // devices
    model_piece = width // devices
    head_cols, model_cols = (
        lax.all_to_all(saved, "context", split_axis=1, concat_axis=0, tiled=True),
        lax.all_to_all(grad_out, "context", split_axis=1, concat_axis=0, tiled=True),
    )
    model_cols = jnp.take(
        model_cols, routed_order(block_route, devices, tok_rows, blocksize), axis=0
    )
    for level in range(levels):
        other = partner(head_cols, "context", level)
        head_cols = join_pair(head_cols, other, myself >> level & 1 == 1, 1)
    for level in range(levels):
        other = partner(model_cols, "context", levels + level)
        model_cols = join_pair(model_cols, other, myself >> levels + level & 1 == 1, 1)
    product = lax.dot_general(
        head_cols, model_cols, (((0,), (0,)), ((), ())), preferred_element_type=jnp.float32
    )
    tile_cols = side * model_piece
    slots = product.astype(jnp.bfloat16).reshape(side, head_piece, tile_cols)
    for level in range(levels):
        upper = myself >> level & 1 == 1
        shaped = slots.reshape(side >> level + 1, 2, 1 << level, head_piece, tile_cols)
        outgoing_half = jnp.where(upper, shaped[:, 0], shaped[:, 1])
        incoming_half = partner(outgoing_half, "context", level)
        first_half = jnp.where(upper, incoming_half, shaped[:, 0])
        second_half = jnp.where(upper, shaped[:, 1], incoming_half)
        slots = jnp.stack((first_half, second_half), axis=1).reshape(side, head_piece, tile_cols)
    arranged = slots.reshape(side, head_piece, side, model_piece).transpose(1, 2, 0, 3)
    return arranged.reshape(head_piece, width)


def solution(mesh):
    return jax.shard_map(
        body,
        mesh=mesh,
        in_specs=(
            P(("groups", "context"), None),
            P(("groups", "context"), None),
            P("groups", None),
        ),
        out_specs=P(("groups", "context"), None),
        check_vma=False,
    )
```

profile of v0, /device:TPU:0, one launch (start us, length us, event | category | flops | bytes accessed | tf_op | source)
XLA Modules:
  0.0 536.0 jit_solution(14579395576065297693)
XLA Ops:
  0.0 3.1 copy.27
  3.1 7.4 %all-to-all-start.1 = ((bf16[128,16,512]{2,0,1:T(8,128)(2,1)}), bf16[128,16,512]{2,0,1:T(8,128)(2,1)S(1)}, u32[]{:S(2)}, u32[]{:S(2)}) async-start(bf16[128,16,512]{2,0,1:T(8,128)(2,1)} %bitcast.62), calls=%async_computation.1 | async-start | bytes 4194304 | tf_op jit(solution)/shard_map/all_to_all | solution.py:38
  10.5 4.1 copy.14
  14.6 37.0 %all-to-all-done.1 = bf16[128,16,512]{2,0,1:T(8,128)(2,1)S(1)} async-done(((bf16[128,16,512]{2,0,1:T(8,128)(2,1)}), bf16[128,16,512]{2,0,1:T(8,128)(2,1)S(1)}, u32[]{:S(2)}, u32[]{:S(2)}) %all-to-all-start.1) | async-done | bytes 2097184 | tf_op jit(solution)/shard_map/all_to_all | solution.py:38
  51.6 11.3 %all-to-all-start = ((bf16[128,16,512]{0,2,1:T(8,128)(2,1)}), bf16[128,16,512]{0,2,1:T(8,128)(2,1)}, u32[]{:S(2)}, u32[]{:S(2)}) async-start(bf16[128,16,512]{0,2,1:T(8,128)(2,1)} %bitcast.61), calls=%async_computation | async-start | bytes 4194304 | tf_op jit(solution)/shard_map/all_to_all | solution.py:37
  63.5 9.2 %gather_fusion = bf16[2048,512]{1,0:T(8,128)(2,1)} fusion(bf16[2048,512]{1,0:T(8,128)(2,1)S(1)} %bitcast.57, s32[2048]{0:T(1024)S(1)} %broadcast_clamp_fusion), kind=kCustom, calls=%fused_computation | custom fusion | bytes 4202496 | tf_op jit(solution)/shard_map/jit(_take)/gather | solution.py:40
  72.7 2.7 broadcast_select_fusion.2
  77.3 26.9 %all-to-all-done = bf16[128,16,512]{0,2,1:T(8,128)(2,1)} async-done(((bf16[128,16,512]{0,2,1:T(8,128)(2,1)}), bf16[128,16,512]{0,2,1:T(8,128)(2,1)}, u32[]{:S(2)}, u32[]{:S(2)}) %all-to-all-start) | async-done | bytes 2097184 | tf_op jit(solution)/shard_map/all_to_all | solution.py:37
  104.2 2.9 copy.15
  107.9 36.9 %collective-permute-done.2 = bf16[2048,512]{1,0:T(8,128)(2,1)} collective-permute-done((bf16[2048,512]{1,0:T(8,128)(2,1)}, bf16[2048,512]{1,0:T(8,128)(2,1)}, u32[]{:S(2)}, u32[]{:S(2)}) %collective-permute-start.2) | collective-permute-done | bytes 2097184 | tf_op jit(solution)/shard_map/ppermute | solution.py:10
  144.7 6.4 %maximum_select_fusion.9 = bf16[2048,1024]{1,0:T(8,128)(2,1)} fusion(bf16[2048,512]{1,0:T(8,128)(2,1)} %broadcast_select_fusion.2, bf16[2048,512]{1,0:T(8,128)(2,1)} %collective-permute-done.2, pred[]{:T(512)S(6)} %eq.17), kind=kLoop, calls=%fused_computation.25 | loop fusion | flops 18874368 | bytes 8388609 | tf_op jit(solution)/shard_map/jit(_where)/select_n | solution.py:23
  151.2 2.5 collective-permute-start.3
  153.7 5.0 maximum_select_fusion.8
  160.3 174.0 %collective-permute-done.3 = bf16[2048,1024]{1,0:T(8,128)(2,1)} collective-permute-done((bf16[2048,1024]{1,0:T(8,128)(2,1)}, bf16[2048,1024]{1,0:T(8,128)(2,1)}, u32[]{:S(2)}, u32[]{:S(2)}) %collective-permute-start.3) | collective-permute-done | bytes 4194336 | tf_op jit(solution)/shard_map/ppermute | solution.py:10
  334.4 30.0 %fusion.13 = bf16[2048,2048]{1,0:T(8,128)(2,1)} fusion(bf16[2048,1024]{1,0:T(8,128)(2,1)} %maximum_select_fusion.9, bf16[2048,1024]{1,0:T(8,128)(2,1)} %collective-permute-done.3, pred[]{:T(512)S(6)} %eq.16, bf16[2048,1024]{1,0:T(8,128)(2,1)} %maximum_select_fusion.8, bf16[2048,1024]{1,0:T(8,128)(2,1)} %collective-permute-done.1, pred[]{:T(512)S(6)} %eq.14), kind=kOutput, calls=%fused_computation.19 | convolution fusion | flops 17259560960 | bytes 25165826 | tf_op jit(solution)/shard_map/dot_general | solution.py:49
  364.4 3.8 broadcast_select_fusion
  368.3 7.1 %collective-permute-done.4 = bf16[2,1,512,2048]{3,2,0,1:T(8,128)(2,1)S(1)} collective-permute-done((bf16[2,1,512,2048]{3,2,0,1:T(8,128)(2,1)S(1)}, bf16[2,1,512,2048]{3,2,0,1:T(8,128)(2,1)S(1)}, u32[]{:S(2)}, u32[]{:S(2)}) %collective-permute-start.4) | collective-permute-done | bytes 4194336 | tf_op jit(solution)/shard_map/ppermute | solution.py:10
  377.7 6.3 %maximum_bitcast_fusion = bf16[1,2,2,512,2048]{4,3,1,2,0:T(8,128)(2,1)} fusion(bf16[2,1,1,512,2048]{4,3,0,2,1:T(8,128)(2,1)} %get-tuple-element.8, bf16[2,1,1,512,2048]{4,3,0,2,1:T(8,128)(2,1)S(1)} %get-tuple-element.7), kind=kLoop, calls=%fused_computation.14 | loop fusion | flops 4194304 | bytes 16777216 | tf_op jit(solution)/shard_map/reshape;reshape | solution.py:56
  384.1 3.8 broadcast_select_fusion.1
  389.5 91.1 %collective-permute-done.5 = bf16[1,2,512,2048]{3,2,1,0:T(8,128)(2,1)S(1)} collective-permute-done((bf16[1,2,512,2048]{3,2,1,0:T(8,128)(2,1)S(1)}, bf16[1,2,512,2048]{3,2,1,0:T(8,128)(2,1)S(1)}, u32[]{:S(2)}, u32[]{:S(2)}) %collective-permute-start.5) | collective-permute-done | bytes 4194336 | tf_op jit(solution)/shard_map/ppermute | solution.py:10
  482.9 6.3 %pad_maximum_fusion = bf16[1,2,2,512,2048]{4,3,2,1,0:T(8,128)(2,1)} fusion(bf16[1,1,2,512,2048]{4,3,2,1,0:T(8,128)(2,1)} %get-tuple-element.6, bf16[1,1,2,512,2048]{4,3,2,1,0:T(8,128)(2,1)S(1)} %get-tuple-element.5), kind=kLoop, calls=%fused_computation.15 | loop fusion | flops 4194304 | bytes 16777216 | tf_op jit(solution)/shard_map/stack | solution.py:61
  489.3 14.5 %reshape_reshape.11 = bf16[4,512,4,512]{3,2,1,0:T(4,128)(2,1)} reshape(bf16[1,2,2,512,2048]{4,3,2,1,0:T(8,128)(2,1)} %pad_maximum_fusion) | data formatting | bytes 16777216 | tf_op jit(solution)/shard_map/reshape;reshape | solution.py:62
  503.8 18.0 %copy.26 = bf16[4,512,4,512]{3,0,2,1:T(4,128)(2,1)} copy(bf16[4,512,4,512]{3,2,1,0:T(4,128)(2,1)} %reshape_reshape.11) | data formatting | bytes 16777216 | tf_op jit(solution)/shard_map/reshape;reshape | solution.py:62
  521.7 14.3 %reshape.94 = bf16[512,8192]{1,0:T(8,128)(2,1)} reshape(bf16[512,4,4,512]{3,2,1,0:T(4,128)(2,1)} %bitcast.60) | data formatting | bytes 16777216 | tf_op jit(solution)/shard_map/reshape | solution.py:63
  (24 shorter events, 11.1 us)
Async XLA Ops:
  3.1 48.5 %all-to-all-start.1 = ((bf16[128,16,512]{2,0,1:T(8,128)(2,1)}), bf16[128,16,512]{2,0,1:T(8,128)(2,1)S(1)}, u32[]{:S(2)}, u32[]{:S(2)}) async-start(bf16[128,16,512]{2,0,1:T(8,128)(2,1)} %bitcast.62), calls=%async_computation.1 | async-start | bytes 4194304 | tf_op jit(solution)/shard_map/all_to_all | solution.py:38
  10.5 52.4 %copy-start.2 = (s32[16,16]{1,0:T(8,128)S(1)}, s32[16,16]{1,0:T(8,128)}, u32[]{:S(2)}) copy-start(s32[16,16]{1,0:T(8,128)} %param.5) | copy-start | bytes 3076
  51.6 52.5 %all-to-all-start = ((bf16[128,16,512]{0,2,1:T(8,128)(2,1)}), bf16[128,16,512]{0,2,1:T(8,128)(2,1)}, u32[]{:S(2)}, u32[]{:S(2)}) async-start(bf16[128,16,512]{0,2,1:T(8,128)(2,1)} %bitcast.61), calls=%async_computation | async-start | bytes 4194304 | tf_op jit(solution)/shard_map/all_to_all | solution.py:37
  75.4 69.3 %collective-permute-start.2 = (bf16[2048,512]{1,0:T(8,128)(2,1)}, bf16[2048,512]{1,0:T(8,128)(2,1)}, u32[]{:S(2)}, u32[]{:S(2)}) collective-permute-start(bf16[2048,512]{1,0:T(8,128)(2,1)} %broadcast_select_fusion.2), channel_id=1, source_target_pairs={{0,4},{1,5},{2,6},{3,7},{4,0},{5,1},{6,2},{7,3},{8,12},{9,13},{10,... | collective-permute-start | bytes 6291464 | tf_op jit(solution)/shard_map/ppermute | solution.py:10
  107.0 46.6 %collective-permute-start = (bf16[2048,512]{1,0:T(8,128)(2,1)S(1)}, bf16[2048,512]{1,0:T(8,128)(2,1)}, u32[]{:S(2)}, u32[]{:S(2)}) collective-permute-start(bf16[2048,512]{1,0:T(8,128)(2,1)S(1)} %bitcast.63), channel_id=1, source_target_pairs={{0,1},{1,0},{2,3},{3,2},{4,5},{5,4},{6,7},{7,6},{8,9},{9,8},{10,11... | collective-permute-start | bytes 6291464 | tf_op jit(solution)/shard_map/ppermute | solution.py:10
  151.2 183.2 %collective-permute-start.3 = (bf16[2048,1024]{1,0:T(8,128)(2,1)}, bf16[2048,1024]{1,0:T(8,128)(2,1)}, u32[]{:S(2)}, u32[]{:S(2)}) collective-permute-start(bf16[2048,1024]{1,0:T(8,128)(2,1)} %maximum_select_fusion.9), channel_id=1, source_target_pairs={{0,8},{1,9},{2,10},{3,11},{4,12},{5,13},{6,14},{7,15},{8,0},{9,1},... | collective-permute-start | bytes 12582920 | tf_op jit(solution)/shard_map/ppermute | solution.py:10
  158.7 175.7 %collective-permute-start.1 = (bf16[2048,1024]{1,0:T(8,128)(2,1)}, bf16[2048,1024]{1,0:T(8,128)(2,1)}, u32[]{:S(2)}, u32[]{:S(2)}) collective-permute-start(bf16[2048,1024]{1,0:T(8,128)(2,1)} %maximum_select_fusion.8), channel_id=1, source_target_pairs={{0,2},{1,3},{2,0},{3,1},{4,6},{5,7},{6,4},{7,5},{8,10},{9,11},{10,... | collective-permute-start | bytes 12582920 | tf_op jit(solution)/shard_map/ppermute | solution.py:10
  364.4 11.1 %copy-start.1 = (bf16[2048,2048]{1,0:T(8,128)(2,1)S(1)}, bf16[2048,2048]{1,0:T(8,128)(2,1)}, u32[]{:S(2)}) copy-start(bf16[2048,2048]{1,0:T(8,128)(2,1)} %fusion.13) | copy-start | bytes 25165828
  368.2 7.2 %collective-permute-start.4 = (bf16[2,1,512,2048]{3,2,0,1:T(8,128)(2,1)S(1)}, bf16[2,1,512,2048]{3,2,0,1:T(8,128)(2,1)S(1)}, u32[]{:S(2)}, u32[]{:S(2)}) collective-permute-start(bf16[2,1,512,2048]{3,2,0,1:T(8,128)(2,1)S(1)} %broadcast_select_fusion), channel_id=1, source_target_pairs={{0,1},{1,0},{2,3},{3,2},{4,5},{5,4},{6,7},{7,6},{8,9},{9,8},{10,11... | collective-permute-start | bytes 12582920 | tf_op jit(solution)/shard_map/ppermute | solution.py:10
  384.1 96.5 %copy-start = (bf16[1,2,2,512,2048]{4,3,1,2,0:T(8,128)(2,1)S(1)}, bf16[1,2,2,512,2048]{4,3,1,2,0:T(8,128)(2,1)}, u32[]{:S(2)}) copy-start(bf16[1,2,2,512,2048]{4,3,1,2,0:T(8,128)(2,1)} %maximum_bitcast_fusion) | copy-start | bytes 25165828
  387.9 92.7 %collective-permute-start.5 = (bf16[1,2,512,2048]{3,2,1,0:T(8,128)(2,1)S(1)}, bf16[1,2,512,2048]{3,2,1,0:T(8,128)(2,1)S(1)}, u32[]{:S(2)}, u32[]{:S(2)}) collective-permute-start(bf16[1,2,512,2048]{3,2,1,0:T(8,128)(2,1)S(1)} %broadcast_select_fusion.1), channel_id=1, source_target_pairs={{0,2},{1,3},{2,0},{3,1},{4,6},{5,7},{6,4},{7,5},{8,10},{9,11},{10,... | collective-permute-start | bytes 12582920 | tf_op jit(solution)/shard_map/ppermute | solution.py:10
where the time goes:
time: 537 us; the launch traced here: 536 us
  waiting for transfers between devices  373 us (69%)
  local copies, waits for them, and re-layouts  66.4 us (12%)
  other arithmetic  39.4 us (7%)
  matrix products  30 us (6%)
  starting transfers between devices  27.1 us (5%)
    ppermute x6, waiting for transfers between devices, partner(): lax.ppermute(array, axis, [(i, i ^ 1 << apart) for i in range(lax.axis_si...  309 us
    all_to_all x1, waiting for transfers between devices, body(): lax.all_to_all(grad_out, 'context', split_axis=1, concat_axis=0, tiled=True)  37 us
    another operation x2, local copies, waits for them, and re-layouts, body(): slots.reshape(side, head_piece, side, model_piece).transpose(1, 2, 0, 3)  32.5 us
    dot_general x1, matrix products, body(): lax.dot_general(head_cols, model_cols, (((0,), (0,)), ((), ())), preferre...  30 us
    all_to_all x1, waiting for transfers between devices, body(): lax.all_to_all(saved, 'context', split_axis=1, concat_axis=0, tiled=True)  26.9 us
    reshape x1, local copies, waits for them, and re-layouts, body(): return arranged.reshape(head_piece, width)  14.3 us
    select_n x2, other arithmetic, join_pair(): return jnp.where(upper, upper_first, lower_first)  11.5 us
    all_to_all x1, starting transfers between devices, body(): lax.all_to_all(saved, 'context', split_axis=1, concat_axis=0, tiled=True)  11.3 us
  transfers between devices with their start and end apart: 8, of which 6 were waited for; matrix products, arithmetic and copies ran while one was open for 6% of the time, Pallas kernels for 0%

commit v1 on v0

--- a/solution.py
+++ b/solution.py
@@ -23,7 +23,7 @@
     return jnp.where(upper, upper_first, lower_first)
 
 
-def body(grad_out, saved, block_route):
+def grid_body(grad_out, saved, block_route):
     devices = lax.axis_size("context")
     side = math.isqrt(devices)
     levels = side.bit_length() - 1
@@ -63,6 +63,31 @@
     return arranged.reshape(head_piece, width)
 
 
+def gather_body(grad_out, saved, block_route):
+    devices = lax.axis_size("context")
+    myself = lax.axis_index("context")
+    tok_rows, width = grad_out.shape
+    inner = saved.shape[1]
+    blocksize = tok_rows // devices
+    route = lax.dynamic_index_in_dim(block_route, myself, 0, keepdims=False)
+    mine = jnp.take(grad_out.reshape(devices, blocksize, width), route, axis=0)
+    grad = lax.all_gather(mine.reshape(tok_rows, width), "context", axis=0, tiled=True)
+    head = lax.all_to_all(saved, "context", split_axis=1, concat_axis=0, tiled=True)
+    head = head.reshape(devices, devices, blocksize, inner // devices).transpose(1, 0, 2, 3)
+    head = head.reshape(devices * tok_rows, inner // devices)
+    product = lax.dot_general(
+        head, grad, (((0,), (0,)), ((), ())), preferred_element_type=jnp.float32
+    )
+    return product.astype(jnp.bfloat16)
+
+
+def body(grad_out, saved, block_route):
+    gathered = lax.axis_size("context") * grad_out.size * grad_out.dtype.itemsize
+    if gathered <= 2 ** 25:
+        return gather_body(grad_out, saved, block_route)
+    return grid_body(grad_out, saved, block_route)
+
+
 def solution(mesh):
     return jax.shard_map(
         body,

time: 537 us -> 273 us (0.51)
  the two profiles are of different devices: /device:TPU:0 before, /device:TPU:9 now
where the time goes in v1:
time: 273 us
  waiting for transfers between devices  130 us (48%)
  blocking collectives  76.4 us (28%)
  matrix products  25.6 us (9%)
  local copies, waits for them, and re-layouts  22.8 us (8%)
  between operations  13.4 us (5%)
  other arithmetic  4.73 us (2%)
    all_gather x1, waiting for transfers between devices, gather_body(): lax.all_gather(mine.reshape(tok_rows, width), 'context', axis=0, tiled=True)  130 us
    all_to_all x1, blocking collectives, gather_body(): lax.all_to_all(saved, 'context', split_axis=1, concat_axis=0, tiled=True)  76.4 us
    dot_general x1, matrix products, gather_body(): lax.dot_general(head, grad, (((0,), (0,)), ((), ())), preferred_element_t...  25.6 us
    convert_element_type x1, local copies, waits for them, and re-layouts, gather_body(): return product.astype(jnp.bfloat16)  12.1 us
  transfers between devices with their start and end apart: 1, of which 1 were waited for; matrix products, arithmetic and copies ran while one was open for 3% of the time, Pallas kernels for 0%

profile of v1, /device:TPU:9, one launch (start us, length us, event | category | flops | bytes accessed | tf_op | source)
XLA Modules:
  0.0 272.8 jit_solution(11795420295757724960)
XLA Ops:
  6.5 0.0 copy-start
  6.5 0.0 all-gather.2.cloned.1.call-start
  6.5 0.8 fusion.1
  7.4 0.7 compare_and_fusion
  8.1 0.1 broadcast_in_dim.14
  8.2 0.1 broadcast_in_dim.15
  8.3 0.0 copy-done
  8.3 2.0 gather_fusion
  10.3 3.2 %bitcast_select_fusion = bf16[128,8192]{1,0:T(8,128)(2,1)} fusion(bf16[16,8,8192]{2,1,0:T(8,128)(2,1)} %gather_fusion, pred[128]{0:T(512)(128)(4,1)S(1)} %broadcast_in_dim.15), kind=kLoop, calls=%fused_computation.3 | loop fusion | flops 1048576 | bytes 4194432 | tf_op jit(solution)/shard_map/jit(_take)/select_n | solution.py:73
  13.5 0.0 copy-start.2
  13.5 0.0 all-gather.2.cloned.1.call-update
  13.5 1.6 copy-done.2
  15.1 2.4 copy.8
  17.5 76.4 %all_to_all.16 = bf16[128,16,512]{0,2,1:T(8,128)(2,1)S(1)} all-to-all(bf16[128,16,512]{0,2,1:T(8,128)(2,1)} %bitcast.22), channel_id=1, replica_groups=mesh['groups'=2,'context'=16] {'context'}, dimensions={1} | all-to-all | bytes 4194304 | tf_op jit(solution)/shard_map/all_to_all | solution.py:75
  93.9 2.6 copy.9
  96.5 2.0 copy.10
  98.5 129.8 %all-gather.2.cloned.1.call-done = bf16[2048,8192]{1,0:T(8,128)(2,1)} async-done(((bf16[128,8192]{1,0:T(8,128)(2,1)}), bf16[2048,8192]{1,0:T(8,128)(2,1)}) %all-gather.2.cloned.1.call-update) | async-done | bytes 33554448 | tf_op jit(solution)/shard_map/all_gather | solution.py:74
  228.3 25.6 %fusion = bf16[512,8192]{0,1:T(8,128)(2,1)} fusion(bf16[2048,8192]{1,0:T(8,128)(2,1)} %all-gather.2.cloned.1.call-done, bf16[2048,512]{1,0:T(8,128)(2,1)S(1)} %bitcast.23), kind=kOutput, calls=%fused_computation.2 | convolution fusion | flops 17184063488 | bytes 44040192 | tf_op jit(solution)/shard_map/dot_general | solution.py:78
  253.9 0.0 copy-start.1
  253.9 12.1 %copy.11 = bf16[512,8192]{1,0:T(8,128)(2,1)} copy(bf16[512,8192]{0,1:T(8,128)(2,1)} %fusion) | data formatting | bytes 16777216 | tf_op jit(solution)/shard_map/convert_element_type | solution.py:81
  266.0 0.0 copy-done.1
  (1 shorter events, 0.0 us)
Async XLA Ops:
  6.5 1.7 copy-start
  6.5 221.7 %all-gather.2.cloned.1.call-start = ((), (), s32[]{:S(2)}) async-start(), calls=%async_computation.1 | async-start | bytes 35651584 | tf_op jit(solution)/shard_map/all_gather | solution.py:74
  13.5 1.6 copy-start.2
  253.9 12.1 %copy-start.1 = (bf16[128,8192]{1,0:T(8,128)(2,1)S(1)}, bf16[128,8192]{1,0:T(8,128)(2,1)}, u32[]{:S(2)}) copy-start(bf16[128,8192]{1,0:T(8,128)(2,1)} %param.3) | copy-start | bytes 6291460
Sparse Core Ops, SparseCore 0:
  13.6 214.6 all-gather.1

commit v2 on v0

--- a/solution.py
+++ b/solution.py
@@ -1,8 +1,11 @@
+import functools
 import math
 
 import jax
 import jax.numpy as jnp
 from jax import lax
+from jax.experimental import pallas as pl
+from jax.experimental.pallas import tpu as pltpu
 from jax.sharding import PartitionSpec as P
 
 
@@ -23,7 +26,7 @@
     return jnp.where(upper, upper_first, lower_first)
 
 
-def body(grad_out, saved, block_route):
+def grid_body(grad_out, saved, block_route):
     devices = lax.axis_size("context")
     side = math.isqrt(devices)
     levels = side.bit_length() - 1
@@ -63,6 +66,310 @@
     return arranged.reshape(head_piece, width)
 
 
+PLANE = 4
+DEPTH = 4
+CHUNKS = 8
+
+
+def fused_kernel(
+    g_ref, s_ref, out_ref,
+    gbuf, sbuf, st, gt, obuf,
+    gp_send, gp_recv, g_local, gz_send, gz_recv,
+    sz_send, sz_recv, s_local, sy_send, sy_recv, sc_send, sc_recv, sf_send, sf_recv,
+    o_send, o_recv, o_local,
+):
+    me = lax.axis_index("context")
+    z, p = me // PLANE, me % PLANE
+    over_y = (p + 2) % PLANE
+    core = p + 1 - 2 * (p % 2)
+    tok, width = g_ref.shape
+    features = s_ref.shape[1]
+    quarter = width // PLANE
+    head = features // DEPTH
+    wide = quarter // CHUNKS
+    rows = head // PLANE
+    part = tok // DEPTH
+
+    def at(zz, pp):
+        return {"context": zz * PLANE + pp}
+
+    def copy(src, dst, send, recv, device):
+        return pltpu.make_async_remote_copy(
+            src_ref=src, dst_ref=dst, send_sem=send, recv_sem=recv,
+            device_id=device, device_id_type=pl.DeviceIdType.MESH,
+        )
+
+    barrier = pltpu.get_barrier_semaphore()
+    for k in range(1, PLANE):
+        pl.semaphore_signal(barrier, inc=1, device_id=at(z, (p + k) % PLANE), device_id_type=pl.DeviceIdType.MESH)
+        pl.semaphore_signal(barrier, inc=1, device_id=at((z + k) % DEPTH, p), device_id_type=pl.DeviceIdType.MESH)
+    pl.semaphore_wait(barrier, PLANE + DEPTH - 2)
+
+    def s_rows(zz, pp):
+        return sbuf.at[pl.ds(pl.multiple_of((zz * PLANE + pp) * tok, tok), tok), :]
+
+    def s_cols(zz):
+        return s_ref.at[:, pl.ds(pl.multiple_of(zz * head, head), head)]
+
+    def s_line(k):
+        other = (z + k) % DEPTH
+        return copy(s_cols(other), s_rows(z, p), sz_send.at[k], sz_recv.at[k], at(other, p))
+
+    def s_line_from(k):
+        other = (z - k + DEPTH) % DEPTH
+        return copy(s_cols(other), s_rows(other, p), sz_send.at[k], sz_recv.at[k], at(other, p))
+
+    def s_own():
+        return pltpu.make_async_copy(s_cols(z), s_rows(z, p), s_local.at[0])
+
+    def source(k):
+        return (z - k + DEPTH) % DEPTH
+
+    def s_across(k, pp):
+        src = s_cols(z) if k == 0 else s_rows(source(k), pp)
+        return copy(src, s_rows(source(k), pp), sy_send.at[k], sy_recv.at[k], at(z, over_y))
+
+    def s_core(k, pp):
+        src = s_cols(z) if k == 0 else s_rows(source(k), pp)
+        return copy(src, s_rows(source(k), pp), sc_send.at[k], sc_recv.at[k], at(z, core))
+
+    def s_pass(k, pp):
+        return copy(s_rows(source(k), pp), s_rows(source(k), pp), sf_send.at[k], sf_recv.at[k], at(z, core))
+
+    def g_cols(pp, j):
+        return g_ref.at[:, pl.ds(pl.multiple_of(pp * quarter + j * wide, wide), wide)]
+
+    def g_rows(j, pp):
+        return gbuf.at[j, z, pl.ds(pl.multiple_of(pp * tok, tok), tok), :]
+
+    def g_plane(j, k):
+        other = (p + k) % PLANE
+        return copy(g_cols(other, j), g_rows(j, p), gp_send.at[j, k], gp_recv.at[j, k], at(z, other))
+
+    def g_plane_from(j, k):
+        other = (p - k + PLANE) % PLANE
+        return copy(g_cols(other, j), g_rows(j, other), gp_send.at[j, k], gp_recv.at[j, k], at(z, other))
+
+    def g_own(j):
+        return pltpu.make_async_copy(g_cols(p, j), g_rows(j, p), g_local.at[j])
+
+    def g_line(j, up, hop):
+        src = z - hop if up else z + hop
+        to = z + 1 if up else z - 1
+        way = 0 if up else 1
+        block = gbuf.at[j, src]
+        return copy(block, block, gz_send.at[way, hop, j], gz_recv.at[way, hop, j], at(to, p))
+
+    def g_line_from(j, up, hop):
+        src = z - hop - 1 if up else z + hop + 1
+        to = z - 1 if up else z + 1
+        way = 0 if up else 1
+        block = gbuf.at[j, src]
+        return copy(block, block, gz_send.at[way, hop, j], gz_recv.at[way, hop, j], at(to, p))
+
+    def sends(up, hop):
+        return (z - hop >= 0) & (z < DEPTH - 1) if up else (z + hop < DEPTH) & (z > 0)
+
+    def takes(up, hop):
+        return z - hop - 1 >= 0 if up else z + hop + 1 < DEPTH
+
+    def own_chunk(j):
+        g_own(j).wait()
+        for k in range(1, PLANE):
+            g_plane_from(j, k).wait_recv()
+        for up in (True, False):
+            @pl.when(sends(up, 0))
+            def _():
+                g_line(j, up, 0).start()
+
+    def take_chunk(j, hop):
+        for up in (True, False):
+            @pl.when(takes(up, hop))
+            def _():
+                g_line_from(j, up, hop).wait_recv()
+            if hop + 1 < DEPTH - 1:
+                @pl.when(sends(up, hop + 1))
+                def _():
+                    g_line(j, up, hop + 1).start()
+
+    def o_piece(j, pp):
+        return obuf.at[j, pl.ds(pl.multiple_of(pp * rows, rows), rows), :]
+
+    def o_cols(pp, j):
+        return out_ref.at[:, pl.ds(pl.multiple_of(pp * quarter + j * wide, wide), wide)]
+
+    def o_to(j, k):
+        other = (p + k) % PLANE
+        return copy(o_piece(j, other), o_cols(p, j), o_send.at[j, k], o_recv.at[j, k], at(z, other))
+
+    def o_from(j, k):
+        other = (p - k + PLANE) % PLANE
+        return copy(o_piece(j, other), o_cols(other, j), o_send.at[j, k], o_recv.at[j, k], at(z, other))
+
+    def o_own(j):
+        return pltpu.make_async_copy(o_piece(j, p), o_cols(p, j), o_local.at[j])
+
+    def compute(j):
+        def place(pair, carry):
+            for zz in range(DEPTH):
+                pieces = [
+                    gbuf[j, zz, pl.ds(pl.multiple_of(pp * tok + pair * 16, 16), 16), :].astype(jnp.float32)
+                    for pp in range(PLANE)
+                ]
+                for half in range(2):
+                    joined = jnp.concatenate([x[half * 8:half * 8 + 8] for x in pieces], axis=0)
+                    base = pl.multiple_of((pair * 2 + half) * tok + zz * part, part)
+                    gt[pl.ds(base, part), :] = joined.astype(jnp.bfloat16)
+            return carry
+
+        lax.fori_loop(0, tok // 16, place, 0)
+
+        def tile(m, carry):
+            owner = (p + 1 + m) % PLANE
+            base = pl.multiple_of(owner * rows, rows)
+            acc = jnp.dot(st[pl.ds(base, rows), :], gt[...], preferred_element_type=jnp.float32)
+            obuf[j, pl.ds(base, rows), :] = acc.astype(jnp.bfloat16)
+            return carry
+
+        lax.fori_loop(0, PLANE, tile, 0)
+        for k in (2, 1, 3):
+            o_to(j, k).start()
+        o_own(j).start()
+
+    s_own().start()
+    g_own(0).start()
+    for k in range(1, PLANE):
+        g_plane(0, k).start()
+    for k in range(1, DEPTH):
+        s_line(k).start()
+
+    def start_chunk(j, carry):
+        g_own(j).start()
+        for k in range(1, PLANE):
+            g_plane(j, k).start()
+        return carry
+
+    lax.fori_loop(1, CHUNKS, start_chunk, 0)
+    s_across(0, p).start()
+    s_core(0, p).start()
+    own_chunk(0)
+    own_chunk(1)
+    for k in (1, 3, 2):
+        s_line_from(k).wait_recv()
+        s_across(k, p).start()
+        s_core(k, p).start()
+    own_chunk(2)
+    take_chunk(0, 0)
+    own_chunk(3)
+    take_chunk(1, 0)
+    take_chunk(0, 1)
+    for k in (0, 1, 3, 2):
+        s_across(k, over_y).wait_recv()
+        s_pass(k, over_y).start()
+    s_own().wait()
+    for k in range(DEPTH):
+        s_core(k, core).wait_recv()
+        s_pass(k, (core + 2) % PLANE).wait_recv()
+
+    def turn(d, carry):
+        base = pl.multiple_of(d * tok, tok)
+        st[:, pl.ds(base, tok)] = sbuf[pl.ds(base, tok), :].T
+        return carry
+
+    lax.fori_loop(0, DEPTH * PLANE, turn, 0)
+
+    def step(j, carry):
+        @pl.when(j + 4 < CHUNKS)
+        def _():
+            own_chunk(j + 4)
+
+        @pl.when(j + 2 < CHUNKS)
+        def _():
+            take_chunk(j + 2, 0)
+
+        @pl.when(j + 1 < CHUNKS)
+        def _():
+            take_chunk(j + 1, 1)
+
+        take_chunk(j, 2)
+        compute(j)
+        return carry
+
+    lax.fori_loop(0, CHUNKS, step, 0)
+
+    for k in range(1, DEPTH):
+        s_line(k).wait_send()
+    for k in range(DEPTH):
+        s_across(k, p).wait_send()
+        s_core(k, p).wait_send()
+        s_pass(k, over_y).wait_send()
+
+    def finish(j, carry):
+        for k in range(1, PLANE):
+            g_plane(j, k).wait_send()
+        for up in (True, False):
+            for hop in range(DEPTH - 1):
+                @pl.when(sends(up, hop))
+                def _():
+                    g_line(j, up, hop).wait_send()
+        for k in range(1, PLANE):
+            o_to(j, k).wait_send()
+            o_from(j, k).wait_recv()
+        o_own(j).wait()
+        return carry
+
+    lax.fori_loop(0, CHUNKS, finish, 0)
+
+
+def fused_body(grad_out, saved, block_route):
+    devices = lax.axis_size("context")
+    myself = lax.axis_index("context")
+    tok, width = grad_out.shape
+    features = saved.shape[1]
+    block = tok // devices
+    route = lax.dynamic_index_in_dim(block_route, myself, 0, keepdims=False)
+    mine = jnp.take(grad_out.reshape(devices, block, width), route, axis=0, mode="clip")
+    mine = mine.reshape(tok, width)
+    tokens = tok * devices
+    head, quarter = features // DEPTH, width // PLANE
+    wide = quarter // CHUNKS
+    dma = pltpu.SemaphoreType.DMA
+    return pl.pallas_call(
+        fused_kernel,
+        out_shape=jax.ShapeDtypeStruct((features // devices, width), jnp.bfloat16),
+        in_specs=[pl.BlockSpec(memory_space=pl.ANY)] * 2,
+        out_specs=pl.BlockSpec(memory_space=pl.ANY),
+        scratch_shapes=[
+            pltpu.VMEM((CHUNKS, DEPTH, tok * PLANE, wide), jnp.bfloat16),
+            pltpu.VMEM((tokens, head), jnp.bfloat16),
+            pltpu.VMEM((head, tokens), jnp.bfloat16),
+            pltpu.VMEM((tokens, wide), jnp.bfloat16),
+            pltpu.VMEM((CHUNKS, head, wide), jnp.bfloat16),
+            dma((CHUNKS, PLANE)), dma((CHUNKS, PLANE)), dma((CHUNKS,)),
+            dma((2, DEPTH, CHUNKS)), dma((2, DEPTH, CHUNKS)),
+            dma((DEPTH,)), dma((DEPTH,)), dma((1,)),
+            dma((DEPTH,)), dma((DEPTH,)), dma((DEPTH,)), dma((DEPTH,)),
+            dma((DEPTH,)), dma((DEPTH,)),
+            dma((CHUNKS, PLANE)), dma((CHUNKS, PLANE)), dma((CHUNKS,)),
+        ],
+        compiler_params=pltpu.CompilerParams(
+            collective_id=0, has_side_effects=True, vmem_limit_bytes=56 * 2 ** 20
+        ),
+        cost_estimate=pl.CostEstimate(
+            flops=2 * head * quarter * tokens, bytes_accessed=2 ** 24, transcendentals=0
+        ),
+    )(mine, saved)
+
+
+def body(grad_out, saved, block_route):
+    devices = lax.axis_size("context")
+    tok, width = grad_out.shape
+    fits = devices == PLANE * DEPTH and tok == devices * 8
+    if fits and width % (PLANE * CHUNKS * 128) == 0 and saved.shape[1] % (devices * 128) == 0:
+        return fused_body(grad_out, saved, block_route)
+    return grid_body(grad_out, saved, block_route)
+
+
 def solution(mesh):
     return jax.shard_map(
         body,

time: 537 us -> 214 us (0.40)
  waiting for transfers between devices: 373 us -> 0 us
  Pallas kernels: 0 us -> 203 us
  local copies, waits for them, and re-layouts: 66.4 us -> 11.4 us
  other arithmetic: 39.4 us -> 0.01 us
  matrix products: 30 us -> 0 us
  starting transfers between devices: 27.1 us -> 0 us
    ppermute x6 -> x0, waiting for transfers between devices: 309 us -> none  [partner(): lax.ppermute(array, axis, [(i, i ^ 1 << apart) for i in range(lax.axis_si...]
    pallas_call x0 -> x1, Pallas kernels: none -> 203 us  [fused_body(): pl.pallas_call(fused_kernel, out_shape=jax.ShapeDtypeStruct((features //...]
    all_to_all x2 -> x0, waiting for transfers between devices: 63.9 us -> none  [the longest x1 37 us: body(): lax.all_to_all(grad_out, 'context', split_axis=1, concat_axis=0, tiled=True)]
    another operation x2 -> x0, local copies, waits for them, and re-layouts: 32.5 us -> none  [body(): slots.reshape(side, head_piece, side, model_piece).transpose(1, 2, 0, 3)]
    dot_general x1 -> x0, matrix products: 30 us -> none  [body(): lax.dot_general(head_cols, model_cols, (((0,), (0,)), ((), ())), preferre...]
    select_n x6 -> x0, other arithmetic: 21.9 us -> none  [the longest x2 11.5 us: join_pair(): return jnp.where(upper, upper_first, lower_first)]
    all_to_all x2 -> x0, starting transfers between devices: 18.6 us -> none  [the longest x1 11.3 us: body(): lax.all_to_all(saved, 'context', split_axis=1, concat_axis=0, tiled=True)]
    another operation x4 -> x0, other arithmetic: 17.3 us -> none  [the longest x3 10.9 us: body(): jnp.stack((first_half, second_half), axis=1)]
  transfers between devices with their start and end apart: 8 -> 0, of which waited for: 6 -> 0; matrix products, arithmetic and copies ran while one was open for 6% -> 0% of each run, Pallas kernels for 0% -> 0%
where the time goes in v2:
time: 214 us
  Pallas kernels  203 us (95%)
  local copies, waits for them, and re-layouts  11.4 us (5%)
    pallas_call x1, Pallas kernels, fused_body(): pl.pallas_call(fused_kernel, out_shape=jax.ShapeDtypeStruct((features //...  203 us
    unnamed x3, local copies, waits for them, and re-layouts  8.54 us

profile of v2, /device:TPU:0, one launch (start us, length us, event | category | flops | bytes accessed | tf_op | source)
XLA Modules:
  0.0 214.0 jit_solution(8088079161598944523)
XLA Ops:
  0.0 0.0 copy-start
  0.0 0.8 dynamic-slice_bitcast_fusion
  0.8 0.8 copy-done
  1.6 2.0 gather_fusion
  3.6 202.7 %shard_map.37 = bf16[512,8192]{1,0:T(8,128)(2,1)} custom-call(bf16[128,8192]{1,0:T(8,128)(2,1)} %bitcast.5, bf16[128,8192]{1,0:T(8,128)(2,1)} %s_ref.1), custom_call_target="tpu_custom_call" | custom-call | flops 17179869184 | bytes 16777216 | tf_op jit(solution)/shard_map/pallas_call | solution.py:337
  206.3 7.8 %copy.5 = bf16[512,8192]{1,0:T(8,128)(2,1)} copy(bf16[512,8192]{1,0:T(8,128)(2,1)} %shard_map.37) | data formatting | bytes 16777216
  (1 shorter events, 0.0 us)
Async XLA Ops:
  0.0 1.6 copy-start

commit v3 on v2

--- a/solution.py
+++ b/solution.py
@@ -68,7 +68,8 @@
 
 PLANE = 4
 DEPTH = 4
-CHUNKS = 8
+CHUNKS = 16
+GROUP = 2
 
 
 def fused_kernel(
@@ -89,6 +90,8 @@
     wide = quarter // CHUNKS
     rows = head // PLANE
     part = tok // DEPTH
+    near = 1 + 2 * (p % 2)
+    far = PLANE - near
 
     def at(zz, pp):
         return {"context": zz * PLANE + pp}
@@ -126,11 +129,11 @@
         return (z - k + DEPTH) % DEPTH
 
     def s_across(k, pp):
-        src = s_cols(z) if k == 0 else s_rows(source(k), pp)
+        src = s_cols(z) if isinstance(k, int) and k == 0 else s_rows(source(k), pp)
         return copy(src, s_rows(source(k), pp), sy_send.at[k], sy_recv.at[k], at(z, over_y))
 
     def s_core(k, pp):
-        src = s_cols(z) if k == 0 else s_rows(source(k), pp)
+        src = s_cols(z) if isinstance(k, int) and k == 0 else s_rows(source(k), pp)
         return copy(src, s_rows(source(k), pp), sc_send.at[k], sc_recv.at[k], at(z, core))
 
     def s_pass(k, pp):
@@ -225,69 +228,106 @@
         lax.fori_loop(0, tok // 16, place, 0)
 
         def tile(m, carry):
-            owner = (p + 1 + m) % PLANE
-            base = pl.multiple_of(owner * rows, rows)
+            k = jnp.where(m == 0, 2, jnp.where(m == 1, far, jnp.where(m == 2, near, 0)))
+            base = pl.multiple_of(((p + k) % PLANE) * rows, rows)
             acc = jnp.dot(st[pl.ds(base, rows), :], gt[...], preferred_element_type=jnp.float32)
             obuf[j, pl.ds(base, rows), :] = acc.astype(jnp.bfloat16)
+
+            @pl.when(m < PLANE - 1)
+            def _():
+                o_to(j, k).start()
+
             return carry
 
         lax.fori_loop(0, PLANE, tile, 0)
-        for k in (2, 1, 3):
-            o_to(j, k).start()
         o_own(j).start()
 
-    s_own().start()
-    g_own(0).start()
-    for k in range(1, PLANE):
-        g_plane(0, k).start()
-    for k in range(1, DEPTH):
-        s_line(k).start()
-
-    def start_chunk(j, carry):
+    def turn(zz, pp):
+        base = pl.multiple_of((zz * PLANE + pp) * tok, tok)
+        st[:, pl.ds(base, tok)] = sbuf[pl.ds(base, tok), :].T
+
+    def spread(k):
+        s_line_from(k).wait_recv()
+        s_across(k, p).start()
+        s_core(k, p).start()
+
+    def collect(k):
+        s_across(k, over_y).wait_recv()
+        s_pass(k, over_y).start()
+        turn(source(k), p)
+        turn(source(k), over_y)
+
+    first = jnp.where(z < DEPTH // 2, 3, 1)
+    second = jnp.where((z == 0) | (z == DEPTH - 1), 2, jnp.where(z == 1, 1, 3))
+    third = 6 - first - second
+
+    def start_chunk(j):
         g_own(j).start()
         for k in range(1, PLANE):
             g_plane(j, k).start()
-        return carry
-
-    lax.fori_loop(1, CHUNKS, start_chunk, 0)
+
+    ahead = jnp.where(z == 0, 3, jnp.where(z == DEPTH - 1, 1, 2))
+    then = jnp.where(z == 1, 3, jnp.where(z == 2, 1, 2))
+    for k in (ahead, then, 6 - ahead - then):
+        s_line(k).start()
+    start_chunk(0)
+    s_own().start()
+    for j in range(1, GROUP):
+        start_chunk(j)
     s_across(0, p).start()
     s_core(0, p).start()
-    own_chunk(0)
-    own_chunk(1)
-    for k in (1, 3, 2):
-        s_line_from(k).wait_recv()
-        s_across(k, p).start()
-        s_core(k, p).start()
-    own_chunk(2)
-    take_chunk(0, 0)
-    own_chunk(3)
-    take_chunk(1, 0)
-    take_chunk(0, 1)
-    for k in (0, 1, 3, 2):
-        s_across(k, over_y).wait_recv()
-        s_pass(k, over_y).start()
+    for j in range(GROUP, 3 * GROUP):
+        start_chunk(j)
+
+    def own_group(i):
+        for j in range(i * GROUP, i * GROUP + GROUP):
+            own_chunk(j)
+
+    def take_group(i, hop):
+        for j in range(i * GROUP, i * GROUP + GROUP):
+            take_chunk(j, hop)
+
+    own_group(0)
+    spread(third)
+    own_group(1)
+    spread(second)
+    spread(first)
+
+    def start_rest(j, carry):
+        start_chunk(j)
+        return carry
+
+    lax.fori_loop(3 * GROUP, CHUNKS, start_rest, 0)
+
+    take_group(0, 0)
+    own_group(2)
     s_own().wait()
-    for k in range(DEPTH):
+    collect(0)
+    take_group(1, 0)
+    collect(first)
+    take_group(0, 1)
+    collect(second)
+    collect(third)
+
+    def gather(k, carry):
         s_core(k, core).wait_recv()
         s_pass(k, (core + 2) % PLANE).wait_recv()
-
-    def turn(d, carry):
-        base = pl.multiple_of(d * tok, tok)
-        st[:, pl.ds(base, tok)] = sbuf[pl.ds(base, tok), :].T
+        turn(source(k), core)
+        turn(source(k), (core + 2) % PLANE)
         return carry
 
-    lax.fori_loop(0, DEPTH * PLANE, turn, 0)
+    lax.fori_loop(0, DEPTH, gather, 0)
 
     def step(j, carry):
-        @pl.when(j + 4 < CHUNKS)
+        @pl.when((j + 3 >= 3 * GROUP) & (j + 3 < CHUNKS))
         def _():
-            own_chunk(j + 4)
-
-        @pl.when(j + 2 < CHUNKS)
+            own_chunk(j + 3)
+
+        @pl.when((j + 2 >= 2 * GROUP) & (j + 2 < CHUNKS))
         def _():
             take_chunk(j + 2, 0)
 
-        @pl.when(j + 1 < CHUNKS)
+        @pl.when((j + 1 >= GROUP) & (j + 1 < CHUNKS))
         def _():
             take_chunk(j + 1, 1)
 

time: 214 us -> 207 us (0.967)
  Pallas kernels: 203 us -> 194 us
    pallas_call x1, Pallas kernels: 203 us -> 194 us  [fused_body(): pl.pallas_call(fused_kernel, out_shape=jax.ShapeDtypeStruct((features //...]
where the time goes in v3:
time: 207 us; the launch traced here: 206 us
  Pallas kernels  194 us (94%)
  local copies, waits for them, and re-layouts  11.4 us (6%)
    pallas_call x1, Pallas kernels, fused_body(): pl.pallas_call(fused_kernel, out_shape=jax.ShapeDtypeStruct((features //...  194 us
    unnamed x3, local copies, waits for them, and re-layouts  8.54 us

profile of v3, /device:TPU:0, one launch (start us, length us, event | category | flops | bytes accessed | tf_op | source)
XLA Modules:
  0.0 205.6 jit_solution(18164418983319889299)
XLA Ops:
  0.0 0.0 copy-start
  0.0 0.8 dynamic-slice_bitcast_fusion
  0.8 0.8 copy-done
  1.6 2.0 gather_fusion
  3.6 194.2 %shard_map.37 = bf16[512,8192]{1,0:T(8,128)(2,1)} custom-call(bf16[128,8192]{1,0:T(8,128)(2,1)} %bitcast.5, bf16[128,8192]{1,0:T(8,128)(2,1)} %s_ref.1), custom_call_target="tpu_custom_call" | custom-call | flops 17179869184 | bytes 16777216 | tf_op jit(solution)/shard_map/pallas_call | solution.py:377
  197.8 7.8 %copy.5 = bf16[512,8192]{1,0:T(8,128)(2,1)} copy(bf16[512,8192]{1,0:T(8,128)(2,1)} %shard_map.37) | data formatting | bytes 16777216
  (1 shorter events, 0.0 us)
Async XLA Ops:
  0.0 1.6 copy-start
